TPU v7x, 32 devices: a whole 2x2x4 slice. The times are simulated.
32 devices in a mesh: dp: 16 (over z, y, x), mp: 2 (over core).
Axes of the slice: x: 2, y: 2, z: 4, core: 2. Of those that a mesh axis runs over, the one named last changes fastest.
Arguments:
- hidden_in: float32 [128, 198, 384], P('dp'), may hold values from -6 to 6
- keep_mask: int32 [128, 198], P('dp'), may hold values from 0 to 1, as said below
- cotangent: float32 [128, 198, 384], P('dp'), may hold values from -6 to 6
- slot_block: int32 [2, 384], replicated, may hold values from 0 to 383, each once within a row
- master: float32 [2, 2, 384, 6, 384], P('mp', None, 'dp'), may hold values from -0.375 to 0.375
- moment_one: float32 [2, 2, 384, 6, 384], P('mp', None, 'dp')
- moment_two: float32 [2, 2, 384, 6, 384], P('mp', None, 'dp'), as said below
- vector_master: float32 [2, 2, 6, 384], P('mp')
- vector_one: float32 [2, 2, 6, 384], P('mp')
- vector_two: float32 [2, 2, 6, 384], P('mp'), as said below
Outputs:
- activations: float32 [128, 198, 384], P('dp')
- input_grad: float32 [128, 198, 384], P('dp')
- matrix_grad: float32 [2, 2, 384, 6, 384], P('mp', None, 'dp')
- matrix_two: float32 [2, 2, 384, 6, 384], P('mp', None, 'dp')
- matrix_new: float32 [2, 2, 384, 6, 384], P('mp', None, 'dp')
- vector_grad: float32 [2, 2, 6, 384], P('mp')
- vector_two_new: float32 [2, 2, 6, 384], P('mp')
- vector_new: float32 [2, 2, 6, 384], P('mp')
Inputs may be any that keep to these rules, and one draw needn't show every extreme that they name: `keep_mask`: positions 0 and 1 of every image are 1; one image in every draw keeps all 198 tokens. `slot_block`: each layer's row is a permutation of the 384 blocks. `moment_two`: positive. `vector_two`: positive.
All inputs are finite; a program needn't handle non-finite values.
Results may differ from a plain program's by a relative error of at most 0.018.
Values may be sent and summed in bfloat16 or wider, within the bound.
A program may use at most 192 MiB of HBM per device.

v0:
```python
from functools import partial

import jax
import jax.numpy as jnp
from jax import lax
from jax.sharding import PartitionSpec as P

HEADS = 6
HD = 64
FF = 1536
STEP = 10


EPS_NORM = 1e-06
BETA_ONE = 0.9
BETA_TWO = 0.999
RATE_MATRIX = 0.003
RATE_VECTOR = 0.01
DECAY_MATRIX = 0.05
EPS_ADAM = 1e-08
NEG_FILL = -1e30


def contract_rows(left, right):
    return lax.dot_general(
        left, right, (((0,), (0,)), ((), ())), preferred_element_type=jnp.float32
    )


def contract_cols(left, right):
    return lax.dot_general(
        left, right, (((1,), (1,)), ((), ())), preferred_element_type=jnp.float32
    )


def layer_norm(values, gain_vec, shift_vec):
    average = jnp.mean(values, -1, keepdims=True)
    centred = values - average
    inv_dev = lax.rsqrt(jnp.mean(centred * centred, -1, keepdims=True) + EPS_NORM)
    normed = centred * inv_dev
    return (normed * gain_vec + shift_vec, normed, inv_dev)


def norm_back(grad_out, normed, inv_dev, gain_vec):
    scaled = grad_out * gain_vec
    grad_in = inv_dev * (
        scaled
        - jnp.mean(scaled, -1, keepdims=True)
        - normed * jnp.mean(scaled * normed, -1, keepdims=True)
    )
    return (grad_in, jnp.sum(grad_out * normed, 0), jnp.sum(grad_out, 0))


def softmax_rows(scores):
    row_top = jnp.max(scores, -1, keepdims=True)
    exponent = jnp.exp(scores - row_top)
    return exponent / jnp.sum(exponent, -1, keepdims=True)


def layer_params(tables, vector_master, shared, number, head_cols, unit_cols):
    rows_now = tables[number]
    vector_rows = vector_master.shape[2]
    flat_bias = vector_master[0, number, : vector_rows - 3].reshape(-1)
    return (
        rows_now[: 3 * head_cols],
        rows_now[3 * head_cols : 4 * head_cols],
        rows_now[4 * head_cols : 4 * head_cols + unit_cols],
        rows_now[4 * head_cols + unit_cols :],
        flat_bias[:head_cols],
        flat_bias[head_cols : 2 * head_cols],
        flat_bias[2 * head_cols :],
        shared[0, number, 0],
        shared[0, number, 1],
        shared[0, number, 2],
        shared[1, number, 0],
        shared[1, number, 1],
        shared[1, number, 2],
    )


def attention_inner(hidden, params, key_mask, images, local_heads):
    head_cols = local_heads * HD
    normed_out, normed, inv_dev = layer_norm(hidden, params[7], params[8])
    normed_low = normed_out.astype(jnp.bfloat16)
    projected = contract_cols(normed_low, params[0])
    queries = (
        (projected[:, :head_cols] + params[4])
        .astype(jnp.bfloat16)
        .reshape(images, -1, local_heads, HD)
    )
    keys_low = (
        projected[:, head_cols : 2 * head_cols]
        .astype(jnp.bfloat16)
        .reshape(images, -1, local_heads, HD)
    )
    values_low = (
        (projected[:, 2 * head_cols :] + params[5])
        .astype(jnp.bfloat16)
        .reshape(images, -1, local_heads, HD)
    )
    raw_scores = jnp.einsum(
        "iqhe,ikhe->ihqk", queries, keys_low, preferred_element_type=jnp.float32
    )
    probabilities = softmax_rows(jnp.where(key_mask, raw_scores * HD ** (-0.5), NEG_FILL))
    probs_low = probabilities.astype(jnp.bfloat16)
    attended = jnp.einsum(
        "ihqk,ikhe->iqhe", probs_low, values_low, preferred_element_type=jnp.float32
    )
    attended = attended.reshape(-1, head_cols).astype(jnp.bfloat16)
    return (
        normed_low,
        normed,
        inv_dev,
        queries,
        keys_low,
        values_low,
        probabilities,
        probs_low,
        attended,
    )


def mlp_inner(hidden, params):
    normed_out, normed, inv_dev = layer_norm(hidden, params[10], params[11])
    normed_low = normed_out.astype(jnp.bfloat16)
    up_pre = contract_cols(normed_low, params[2]) + params[6]
    activated = jax.nn.gelu(up_pre, approximate=False).astype(jnp.bfloat16)
    return (normed_low, normed, inv_dev, up_pre, activated)


def mlp_back(grad_out, saved, params):
    normed_low, normed, inv_dev, up_pre, activated = saved
    grad_low = grad_out.astype(jnp.bfloat16)
    grad_bias_down = jnp.sum(grad_low.astype(jnp.float32), 0)
    grad_down = contract_rows(activated, grad_low)
    grad_act = contract_cols(grad_low, params[3])
    gelu_back = jax.vjp(partial(jax.nn.gelu, approximate=False), up_pre)[1]
    grad_pre = gelu_back(grad_act)[0].astype(jnp.bfloat16)
    grad_bias_up = jnp.sum(grad_pre.astype(jnp.float32), 0)
    grad_up = contract_rows(grad_pre, normed_low)
    partial_in = jnp.dot(grad_pre, params[2], preferred_element_type=jnp.float32)
    return (partial_in, grad_up, grad_down, grad_bias_up, grad_bias_down)


def attention_back(grad_out, saved, params, key_mask, local_heads):
    (
        normed_low,
        normed,
        inv_dev,
        queries,
        keys_low,
        values_low,
        probabilities,
        probs_low,
        attended,
    ) = saved
    head_cols = local_heads * HD
    tokens = normed_low.shape[0]
    grad_low = grad_out.astype(jnp.bfloat16)
    grad_bias_out = jnp.sum(grad_low.astype(jnp.float32), 0)
    grad_outproj = contract_rows(attended, grad_low)
    grad_att = contract_cols(grad_low, params[1]).astype(jnp.bfloat16).reshape(queries.shape)
    grad_values = jnp.einsum(
        "ihqk,iqhe->ikhe", probs_low, grad_att, preferred_element_type=jnp.float32
    ).astype(jnp.bfloat16)
    grad_probs = jnp.einsum(
        "iqhe,ikhe->ihqk", grad_att, values_low, preferred_element_type=jnp.float32
    )
    grad_scores = probabilities * (
        grad_probs - jnp.sum(probabilities * grad_probs, -1, keepdims=True)
    )
    grad_raw = (jnp.where(key_mask, grad_scores, 0.0) * HD ** (-0.5)).astype(jnp.bfloat16)
    grad_queries = (
        jnp.einsum("ihqk,ikhe->iqhe", grad_raw, keys_low, preferred_element_type=jnp.float32)
        .astype(jnp.bfloat16)
        .reshape(tokens, head_cols)
    )
    grad_keys = (
        jnp.einsum("ihqk,iqhe->ikhe", grad_raw, queries, preferred_element_type=jnp.float32)
        .astype(jnp.bfloat16)
        .reshape(tokens, head_cols)
    )
    grad_values = grad_values.reshape(tokens, head_cols)
    grad_proj = jnp.concatenate([grad_queries, grad_keys, grad_values], 1)
    grad_qkv_rows = contract_rows(grad_proj, normed_low)
    grad_bias_query = jnp.sum(grad_queries.astype(jnp.float32), 0)
    grad_bias_value = jnp.sum(grad_values.astype(jnp.float32), 0)
    partial_in = jnp.dot(grad_proj, params[0], preferred_element_type=jnp.float32)
    return (
        partial_in,
        grad_qkv_rows,
        grad_outproj,
        grad_bias_query,
        grad_bias_value,
        grad_bias_out,
    )


def adam_step(weight, grad_sum, first_old, second_old, rate, decay):
    first_new = BETA_ONE * first_old + (1.0 - BETA_ONE) * grad_sum
    second_new = BETA_TWO * second_old + (1.0 - BETA_TWO) * grad_sum * grad_sum
    first_hat = first_new / (1.0 - BETA_ONE**STEP)
    second_hat = second_new / (1.0 - BETA_TWO**STEP)
    return (
        second_new,
        weight - rate * (first_hat / (jnp.sqrt(second_hat) + EPS_ADAM) + decay * weight),
    )


def shards(
    hidden_in,
    keep_mask,
    cotangent,
    slot_block,
    master,
    moment_one,
    moment_two,
    vector_master,
    vector_one,
    vector_two,
):
    images, seq_len, features = hidden_in.shape
    tokens = images * seq_len
    halves = lax.axis_size("mp")
    local_heads = HEADS // halves
    head_cols = local_heads * HD
    unit_cols = FF // halves
    layers = master.shape[1]
    blocks = slot_block.shape[1]
    block_rows = master.shape[3]
    vector_rows = vector_master.shape[2]
    layer_ids = jnp.arange(layers, dtype=jnp.int32)[:, None]
    inverse = (
        jnp.zeros((layers, blocks), jnp.int32)
        .at[layer_ids, slot_block]
        .set(jnp.broadcast_to(jnp.arange(blocks, dtype=jnp.int32), (layers, blocks)))
    )
    gathered = lax.all_gather(master.astype(jnp.bfloat16), "dp", axis=2, tiled=True)
    tables = gathered[0][layer_ids, inverse].reshape(layers, blocks * block_rows, features)
    shared = lax.all_gather(vector_master[:, :, vector_rows - 3 :], "mp", axis=0, tiled=True)
    keep_float = keep_mask.astype(jnp.float32).reshape(tokens, 1)
    key_mask = (keep_mask > 0)[:, None, None, :]
    hidden = hidden_in.reshape(tokens, features)
    stash = []
    for number in range(layers):
        params = layer_params(tables, vector_master, shared, number, head_cols, unit_cols)
        attn_saved = attention_inner(hidden, params, key_mask, images, local_heads)
        attn_sum = lax.psum(
            jnp.dot(attn_saved[8], params[1], preferred_element_type=jnp.float32), "mp"
        )
        middle = hidden + (attn_sum + params[9])
        mlp_saved = mlp_inner(middle, params)
        mlp_sum = lax.psum(
            jnp.dot(mlp_saved[4], params[3], preferred_element_type=jnp.float32), "mp"
        )
        stash.append((hidden, middle))
        hidden = middle + (mlp_sum + params[12])
    activations = (hidden * keep_float).reshape(images, seq_len, features)
    grad_hidden = cotangent.reshape(tokens, features) * keep_float
    table_grads = [None] * layers
    vector_grads = [None] * layers
    first_half = lax.axis_index("mp") == 0
    for number in reversed(range(layers)):
        params = layer_params(tables, vector_master, shared, number, head_cols, unit_cols)
        hidden_at, middle_at = stash[number]
        attn_saved = attention_inner(hidden_at, params, key_mask, images, local_heads)
        mlp_saved = mlp_inner(middle_at, params)
        partial_mlp, grad_up, grad_down, grad_bias_up, grad_bias_down = mlp_back(
            grad_hidden, mlp_saved, params
        )
        grad_normed_b = lax.psum(partial_mlp, "mp")
        grad_from_b, grad_gain_two, grad_shift_two = norm_back(
            grad_normed_b, mlp_saved[1], mlp_saved[2], params[10]
        )
        grad_middle = grad_hidden + grad_from_b
        (
            partial_attn,
            grad_qkv_rows,
            grad_outproj,
            grad_bias_query,
            grad_bias_value,
            grad_bias_out,
        ) = attention_back(grad_middle, attn_saved, params, key_mask, local_heads)
        grad_normed_a = lax.psum(partial_attn, "mp")
        grad_from_a, grad_gain_one, grad_shift_one = norm_back(
            grad_normed_a, attn_saved[1], attn_saved[2], params[7]
        )
        grad_hidden = grad_middle + grad_from_a
        rows_grad = jnp.concatenate([grad_qkv_rows, grad_outproj, grad_up, grad_down], 0)
        table_grads[number] = rows_grad
        local_vectors = jnp.concatenate([grad_bias_query, grad_bias_value, grad_bias_up]).reshape(
            vector_rows - 3, features
        )
        own_vectors = jnp.where(
            first_half,
            jnp.stack([grad_gain_one, grad_shift_one, grad_bias_out]),
            jnp.stack([grad_gain_two, grad_shift_two, grad_bias_down]),
        )
        vector_grads[number] = jnp.concatenate([local_vectors, own_vectors], 0)
    whole = jnp.stack(table_grads, 0).reshape(layers, blocks, block_rows, features)[
        layer_ids, slot_block
    ]
    matrix_grad = lax.psum_scatter(whole[None], "dp", scatter_dimension=2, tiled=True)
    vector_grad = lax.psum(jnp.stack(vector_grads, 0)[None], "dp")
    matrix_two, matrix_new = adam_step(
        master, matrix_grad, moment_one, moment_two, RATE_MATRIX, DECAY_MATRIX
    )
    vector_two_new, vector_new = adam_step(
        vector_master, vector_grad, vector_one, vector_two, RATE_VECTOR, 0.0
    )
    input_grad = grad_hidden.reshape(images, seq_len, features)
    return (
        activations,
        input_grad,
        matrix_grad,
        matrix_two,
        matrix_new,
        vector_grad,
        vector_two_new,
        vector_new,
    )


def solution(mesh):
    placed = (
        P("dp", None, None),
        P("dp", None),
        P("dp", None, None),
        P(),
        P("mp", None, "dp", None, None),
        P("mp", None, "dp", None, None),
        P("mp", None, "dp", None, None),
        P("mp", None, None, None),
        P("mp", None, None, None),
        P("mp", None, None, None),
    )
    return jax.shard_map(
        shards,
        mesh=mesh,
        in_specs=placed,
        out_specs=(
            P("dp", None, None),
            P("dp", None, None),
            P("mp", None, "dp", None, None),
            P("mp", None, "dp", None, None),
            P("mp", None, "dp", None, None),
            P("mp", None, None, None),
            P("mp", None, None, None),
            P("mp", None, None, None),
        ),
        check_vma=False,
    )
```

profile of v0, /device:TPU:0, one launch (start us, length us, event | category | flops | bytes accessed | tf_op | source)
XLA Modules:
  0.0 694.9 jit_solution(15417661834928324442)
XLA Ops:
  19.9 36.3 %scatter_fusion = s32[2,384]{1,0:T(2,128)S(1)} fusion(s32[2,384]{1,0:T(2,128)S(1)} %broadcast.355, s32[768]{0:T(1024)S(1)} %reshape.309, s32[768]{0:T(1024)S(1)} %reshape.311), kind=kCustom, calls=%fused_computation.2 | custom fusion | bytes 15360 | tf_op jit(solution)/shard_map/scatter | solution.py:236
  56.4 29.3 %all-gather.2.cloned.1.call-done = bf16[1,2,384,6,384]{4,2,3,1,0:T(8,128)(2,1)} async-done(((bf16[1,2,24,6,384]{4,2,3,1,0:T(8,128)(2,1)}), bf16[1,2,384,6,384]{4,2,3,1,0:T(8,128)(2,1)}) %all-gather.2.cloned.1.call-update) | async-done | bytes 3538960 | tf_op jit(solution)/shard_map/all_gather | solution.py:238
  85.7 6.4 copy.156
  92.1 10.1 %gather_fusion = bf16[768,6,384]{2,1,0:T(8,128)(2,1)} fusion(bf16[2,384,6,384]{3,2,1,0:T(8,128)(2,1)} %copy.156, s32[768]{0:T(1024)S(1)} %reshape.297), kind=kCustom, calls=%fused_computation | custom fusion | bytes 7084032 | tf_op jit(solution)/shard_map/gather | solution.py:239
  143.4 9.4 %all-reduce.9.cloned.1.call-done = f32[1584,384]{1,0:T(8,128)} async-done(((f32[1584,384]{1,0:T(8,128)}), f32[1584,384]{1,0:T(8,128)}) %all-reduce.9.cloned.1.call-update) | async-done | bytes 2433040 | tf_op jit(solution)/shard_map/psum | solution.py:248
  156.3 13.6 %multiply_convert_fusion.3 = (bf16[1584,768]{1,0:T(8,128)(2,1)S(1)}, f32[1584,768]{1,0:T(8,128)}, f32[1584,768]{1,0:T(8,128)}) fusion(f32[768]{0:T(1024)S(1)} %add.317, bf16[768,384]{1,0:T(8,128)(2,1)S(1)} %copy-done.50, f32[1584,384]{1,0:T(8,128)S(1)} %get-tuple-element.93, f32[384]{0:T(512)S(1)} %get-tuple-element.63, f32[384]{0:T(512)S(1)} %get-tuple-element.64, ...), kind=kOutput, calls=%fused_computation.39 | convolution fusion | flops 1017612288 | bytes 15206784 | tf_op jit(solution)/shard_map/dot_general | solution.py:31
  175.6 21.8 %all-reduce.11.cloned.1.call-done = f32[1584,384]{1,0:T(8,128)} async-done(((f32[1584,384]{1,0:T(8,128)}), f32[1584,384]{1,0:T(8,128)}) %all-reduce.11.cloned.1.call-update) | async-done | bytes 2433040 | tf_op jit(solution)/shard_map/psum | solution.py:253
  235.3 13.3 %all-reduce.13.cloned.1.call-done = f32[1584,384]{1,0:T(8,128)} async-done(((f32[1584,384]{1,0:T(8,128)}), f32[1584,384]{1,0:T(8,128)}) %all-reduce.13.cloned.1.call-update) | async-done | bytes 2433040 | tf_op jit(solution)/shard_map/psum | solution.py:248
  252.1 13.5 %multiply_convert_fusion.2 = (bf16[1584,768]{1,0:T(8,128)(2,1)}, f32[1584,768]{1,0:T(8,128)S(1)}, f32[1584,768]{1,0:T(8,128)S(1)}) fusion(f32[768]{0:T(1024)S(1)} %add.340, bf16[768,384]{1,0:T(8,128)(2,1)S(1)} %copy-done.56, f32[1584,384]{1,0:T(8,128)S(1)} %get-tuple-element.87, f32[384]{0:T(512)S(1)} %get-tuple-element.57, f32[384]{0:T(512)S(1)} %get-tuple-element.58, ...), kind=kOutput, calls=%fused_computation.26 | convolution fusion | flops 1017612288 | bytes 15206784 | tf_op jit(solution)/shard_map/dot_general | solution.py:31
  279.7 16.3 %all-reduce.15.cloned.1.call-done = f32[1584,384]{1,0:T(8,128)} async-done(((f32[1584,384]{1,0:T(8,128)}), f32[1584,384]{1,0:T(8,128)}) %all-reduce.15.cloned.1.call-update) | async-done | bytes 2433040 | tf_op jit(solution)/shard_map/psum | solution.py:271
  316.0 9.7 %fusion.62 = bf16[8,198,3,64]{1,3,2,0:T(8,128)(2,1)} fusion(f32[8,3,198,198]{2,3,1,0:T(8,128)} %fusion.93, pred[8,198]{1,0:T(8,128)(4,1)S(1)} %broadcast_compare_fusion, bf16[8,198,3,64]{1,0,3,2:T(8,128)(2,1)} %reshape.282, f32[8,3,198,198]{2,3,1,0:T(8,128)} %get-tuple-element.118, f32[8,3,198]{2,1,0:T(4,128)S(1)} %copy-done.93), kind=kOutput, calls=%fused_computation.131 | convolution fusion | flops 128270936 | bytes 8764272 | tf_op jit(solution)/shard_map/ihqk,iqhe->ikhe/dot_general | solution.py:179
  325.7 9.9 %convert_reduce_fusion.7 = (f32[3,64]{1,0:T(4,128)S(1)}, bf16[8,198,3,64]{1,3,2,0:T(8,128)(2,1)}) fusion(f32[8,3,198,198]{2,3,1,0:T(8,128)} %fusion.93, pred[8,198]{1,0:T(8,128)(4,1)S(1)} %broadcast_compare_fusion, f32[8,3,198,198]{2,3,1,0:T(8,128)} %get-tuple-element.118, f32[8,3,198]{2,1,0:T(4,128)S(1)} %copy-done.93, ...), kind=kOutput, calls=%fused_computation.116 | convolution fusion | flops 128879000 | bytes 8765040 | tf_op jit(solution)/shard_map/ihqk,ikhe->iqhe/dot_general | solution.py:174
  352.3 23.0 %all-reduce.17.cloned.1.call-done = f32[1584,384]{1,0:T(8,128)} async-done(((f32[1584,384]{1,0:T(8,128)}), f32[1584,384]{1,0:T(8,128)}) %all-reduce.17.cloned.1.call-update) | async-done | bytes 2433040 | tf_op jit(solution)/shard_map/psum | solution.py:284
  380.2 5.3 convert_reduce_fusion.1
  395.5 17.5 %all-reduce.19.cloned.1.call-done = f32[1584,384]{1,0:T(8,128)} async-done(((f32[1584,384]{1,0:T(8,128)}), f32[1584,384]{1,0:T(8,128)}) %all-reduce.19.cloned.1.call-update) | async-done | bytes 2433040 | tf_op jit(solution)/shard_map/psum | solution.py:271
  432.9 9.8 %convert_reduce_fusion.9 = (f32[3,64]{1,0:T(4,128)S(1)}, bf16[8,198,3,64]{1,3,2,0:T(8,128)(2,1)}) fusion(f32[8,3,198,198]{2,3,1,0:T(8,128)} %fusion.90, pred[8,198]{1,0:T(8,128)(4,1)S(1)} %broadcast_compare_fusion, f32[8,3,198,198]{2,3,1,0:T(8,128)} %copy-done.89, f32[8,3,198]{2,1,0:T(4,128)S(1)} %copy-done.91, bf16[8,198,3,64]{1,0,3,2:T(8,128)(2,1)} %reshape.280), kind=kOutput, calls=%fused_computation.118 | convolution fusion | flops 128879000 | bytes 8765040 | tf_op jit(solution)/shard_map/ihqk,ikhe->iqhe/dot_general | solution.py:174
  442.7 9.4 %fusion.68 = bf16[8,198,3,64]{1,3,2,0:T(8,128)(2,1)} fusion(f32[8,3,198,198]{2,3,1,0:T(8,128)} %fusion.90, pred[8,198]{1,0:T(8,128)(4,1)S(1)} %broadcast_compare_fusion, bf16[8,198,3,64]{1,0,3,2:T(8,128)(2,1)S(1)} %copy-done.28, f32[8,3,198,198]{2,3,1,0:T(8,128)} %copy-done.89, f32[8,3,198]{2,1,0:T(4,128)S(1)} %copy-done.91), kind=kOutput, calls=%fused_computation.133 | convolution fusion | flops 128270936 | bytes 8764272 | tf_op jit(solution)/shard_map/ihqk,iqhe->ikhe/dot_general | solution.py:179
  496.9 5.2 stack.66
  502.2 8.3 %pad_maximum_fusion = f32[2,384,6,384]{3,2,1,0:T(8,128)} fusion(f32[1,384,6,384]{3,2,1,0:T(8,128)} %stack.67, f32[1,384,6,384]{3,2,1,0:T(8,128)} %stack.66), kind=kLoop, calls=%fused_computation.7 | loop fusion | flops 1769472 | bytes 14155776 | tf_op jit(solution)/shard_map/stack | solution.py:300
  510.5 12.7 %gather_fusion.1 = f32[768,6,384]{2,1,0:T(8,128)} fusion(f32[2,384,6,384]{3,2,1,0:T(8,128)} %pad_maximum_fusion, s32[768]{0:T(1024)S(1)} %reshape.303), kind=kCustom, calls=%fused_computation.1 | custom fusion | bytes 14161920 | tf_op jit(solution)/shard_map/gather | solution.py:300
  523.2 8.0 %copy.192 = f32[768,6,384]{2,0,1:T(8,128)} copy(f32[768,6,384]{2,1,0:T(8,128)} %gather_fusion.1) | data formatting | bytes 14155776 | tf_op jit(solution)/shard_map/gather | solution.py:300
  532.8 5.6 multiply_reduce_fusion.5
  548.3 78.2 %psum.71 = f32[1,2,6,384]{3,1,2,0:T(2,128)S(1)} all-reduce(f32[1,2,6,384]{3,1,2,0:T(2,128)S(1)} %maximum_bitcast_fusion), channel_id=1, replica_groups=mesh['dp'=16,'mp'=2] {'dp'}, use_global_device_ids=true, to_apply=%region_50.51 | all-reduce | flops 4608 | bytes 36864 | tf_op jit(solution)/shard_map/psum | solution.py:304
  627.2 56.7 %reduce-scatter.2.cloned.1.call-done = f32[1,2,24,6,384]{4,2,1,3,0:T(8,128)} async-done(((f32[1,2,384,6,384]{4,2,1,3,0:T(8,128)}), f32[1,2,24,6,384]{4,2,1,3,0:T(8,128)}) %reduce-scatter.2.cloned.1.call-update) | async-done | bytes 442384 | tf_op jit(solution)/shard_map/reduce_scatter | solution.py:303
  (399 shorter events, 249.9 us)
Async XLA Ops:
  7.2 78.5 %all-gather.2.cloned.1.call-start = ((), (), s32[]{:S(2)}) async-start(), calls=%async_computation.1 | async-start | bytes 3760128 | tf_op jit(solution)/shard_map/all_gather | solution.py:238
  9.1 143.7 %all-reduce.9.cloned.1.call-start = ((), (), s32[]{:S(2)}) async-start(), calls=%async_computation.2 | async-start | bytes 4866048 | tf_op jit(solution)/shard_map/psum | solution.py:248
  15.3 140.1 %copy-start.82 = (f32[384]{0:T(512)}, f32[384]{0:T(512)S(1)}, u32[]{:S(2)}) copy-start(f32[384]{0:T(512)S(1)} %get-tuple-element.63) | copy-start | bytes 4612
  15.3 185.5 %copy-start.78 = (f32[384]{0:T(512)}, f32[384]{0:T(512)S(1)}, u32[]{:S(2)}) copy-start(f32[384]{0:T(512)S(1)} %get-tuple-element.60) | copy-start | bytes 4612
  19.9 36.4 %copy-start.62 = (f32[1,2,6,384]{3,1,2,0:T(2,128)S(1)}, f32[1,2,6,384]{3,1,2,0:T(2,128)}, u32[]{:S(2)}) copy-start(f32[1,2,6,384]{3,1,2,0:T(2,128)} %param.17) | copy-start | bytes 55300
  19.9 36.5 %copy-start.69 = (s32[8,198]{1,0:T(8,128)S(1)}, s32[8,198]{1,0:T(8,128)}, u32[]{:S(2)}) copy-start(s32[8,198]{1,0:T(8,128)} %param.11) | copy-start | bytes 19012
  132.1 65.4 %all-reduce.11.cloned.1.call-start = ((), (), s32[]{:S(2)}) async-start(), calls=%async_computation.3 | async-start | bytes 4866048 | tf_op jit(solution)/shard_map/psum | solution.py:253
  135.8 16.9 %copy-start.14 = (f32[1584,384]{1,0:T(8,128)}, f32[1584,384]{1,0:T(8,128)S(1)}, u32[]{:S(2)}) copy-start(f32[1584,384]{1,0:T(8,128)S(1)} %reshape.277) | copy-start | bytes 7299076
  154.8 15.1 %copy-start.4 = (f32[1584,384]{1,0:T(8,128)}, f32[1584,384]{1,0:T(8,128)S(1)}, u32[]{:S(2)}) copy-start(f32[1584,384]{1,0:T(8,128)S(1)} %get-tuple-element.93) | copy-start | bytes 7299076
  156.3 15.1 %copy-start.52 = (bf16[768,384]{1,0:T(8,128)(2,1)S(1)}, bf16[768,384]{1,0:T(8,128)(2,1)}, u32[]{:S(2)}) copy-start(bf16[768,384]{1,0:T(8,128)(2,1)} %slice.199) | copy-start | bytes 1769476
  174.4 74.2 %all-reduce.13.cloned.1.call-start = ((), (), s32[]{:S(2)}) async-start(), calls=%async_computation.4 | async-start | bytes 4866048 | tf_op jit(solution)/shard_map/psum | solution.py:248
  175.5 25.3 %copy-start.39 = (bf16[576,384]{1,0:T(8,128)(2,1)}, bf16[576,384]{1,0:T(8,128)(2,1)S(1)}, u32[]{:S(2)}) copy-start(bf16[576,384]{1,0:T(8,128)(2,1)S(1)} %slice.204) | copy-start | bytes 1327108
  225.5 70.5 %all-reduce.15.cloned.1.call-start = ((), (), s32[]{:S(2)}) async-start(), calls=%async_computation.5 | async-start | bytes 4866048 | tf_op jit(solution)/shard_map/psum | solution.py:271
  250.7 14.9 %copy-start = (f32[1584,384]{1,0:T(8,128)}, f32[1584,384]{1,0:T(8,128)S(1)}, u32[]{:S(2)}) copy-start(f32[1584,384]{1,0:T(8,128)S(1)} %get-tuple-element.87) | copy-start | bytes 7299076
  272.9 102.4 %all-reduce.17.cloned.1.call-start = ((), (), s32[]{:S(2)}) async-start(), calls=%async_computation.6 | async-start | bytes 4866048 | tf_op jit(solution)/shard_map/psum | solution.py:284
  352.2 60.7 %all-reduce.19.cloned.1.call-start = ((), (), s32[]{:S(2)}) async-start(), calls=%async_computation.7 | async-start | bytes 4866048 | tf_op jit(solution)/shard_map/psum | solution.py:271
  389.8 142.6 %all-reduce.21.cloned.1.call-start = ((), (), s32[]{:S(2)}) async-start(), calls=%async_computation.9 | async-start | bytes 9732096 | tf_op jit(solution)/shard_map/psum | solution.py:253
  468.7 215.3 %reduce-scatter.2.cloned.1.call-start = ((), (), s32[]{:S(2)}) async-start(), calls=%async_computation.8 | async-start | bytes 7520256 | tf_op jit(solution)/shard_map/reduce_scatter | solution.py:303
  546.4 80.1 %copy-start.63 = (f32[1,2,6,384]{3,1,2,0:T(2,128)S(1)}, f32[1,2,6,384]{3,1,2,0:T(2,128)}, u32[]{:S(2)}) copy-start(f32[1,2,6,384]{3,1,2,0:T(2,128)} %param.17) | copy-start | bytes 55300
  546.4 80.1 %copy-start.72 = (f32[1,2,6,384]{3,1,2,0:T(2,128)S(1)}, f32[1,2,6,384]{3,1,2,0:T(2,128)}, u32[]{:S(2)}) copy-start(f32[1,2,6,384]{3,1,2,0:T(2,128)} %param.18) | copy-start | bytes 55300
  546.4 80.1 %copy-start.73 = (f32[1,2,6,384]{3,1,2,0:T(2,128)S(1)}, f32[1,2,6,384]{3,1,2,0:T(2,128)}, u32[]{:S(2)}) copy-start(f32[1,2,6,384]{3,1,2,0:T(2,128)} %param.19) | copy-start | bytes 55300
  546.4 137.5 %copy-start.42 = (f32[1,2,24,6,384]{4,2,3,1,0:T(8,128)S(1)}, f32[1,2,24,6,384]{4,2,3,1,0:T(8,128)}, u32[]{:S(2)}) copy-start(f32[1,2,24,6,384]{4,2,3,1,0:T(8,128)} %param.14) | copy-start | bytes 1327108
  546.4 137.5 %copy-start.57 = (f32[1,2,24,6,384]{4,2,3,1,0:T(8,128)S(1)}, f32[1,2,24,6,384]{4,2,3,1,0:T(8,128)}, u32[]{:S(2)}) copy-start(f32[1,2,24,6,384]{4,2,3,1,0:T(8,128)} %param.15) | copy-start | bytes 1327108
  626.5 61.3 %copy-start.64 = (f32[1,2,6,384]{3,1,2,0:T(2,128)}, f32[1,2,6,384]{3,1,2,0:T(2,128)S(1)}, u32[]{:S(2)}) copy-start(f32[1,2,6,384]{3,1,2,0:T(2,128)S(1)} %psum.71) | copy-start | bytes 55300
  (82 other events, 272.3 us)
Sparse Core Ops, SparseCore 0:
  11.3 74.3 all-gather.1
  132.2 20.5 all-reduce.8
  174.5 22.9 all-reduce.10
  225.6 22.9 all-reduce.12
  273.0 22.9 all-reduce.14
  352.4 22.9 all-reduce.16
  389.9 22.9 all-reduce.18
  468.8 30.5 all-reduce.20
  531.3 152.6 reduce-scatter.1
where the time goes:
time: 706 us; the launch traced here: 695 us
  local copies, waits for them, and re-layouts  202 us (29%)
  waiting for transfers between devices  187 us (26%)
  matrix products  142 us (20%)
  blocking collectives  80.1 us (11%)
  other arithmetic  65.8 us (9%)
  between operations  15.6 us (2%)
    psum x1, blocking collectives, shards(): vector_grad = lax.psum(jnp.stack(vector_grads, 0)[None], 'dp')  78.2 us
    reduce_scatter x1, waiting for transfers between devices, shards(): lax.psum_scatter(whole[None], 'dp', scatter_dimension=2, tiled=True)  56.7 us
    dot_general x8, matrix products, contract_cols(): lax.dot_general(left, right, (((1,), (1,)), ((), ())), preferred_element_...  42.3 us
    unnamed x203, local copies, waits for them, and re-layouts  36.9 us
    scatter x1, local copies, waits for them, and re-layouts, shards(): inverse = jnp.zeros((layers, blocks), jnp.int32).at[layer_ids, slot_block...  36.3 us
    psum x2, waiting for transfers between devices, shards(): grad_normed_b = lax.psum(partial_mlp, 'mp')  33.8 us
    all_gather x1, waiting for transfers between devices, shards(): lax.all_gather(master.astype(jnp.bfloat16), 'dp', axis=2, tiled=True)  29.3 us
    psum x1, waiting for transfers between devices, shards(): grad_normed_a = lax.psum(partial_attn, 'mp')  23 us
  transfers between devices with their start and end apart: 9, of which 8 were waited for; matrix products, arithmetic and copies ran while one was open for 22% of the time, Pallas kernels for 0%

commit v1 on v0

v1 whole, which is shorter than its diff:
```python
import functools

import jax
import jax.numpy as jnp
from jax import lax
from jax.experimental import pallas as pl
from jax.experimental.pallas import tpu as pltpu
from jax.sharding import PartitionSpec as P

HEADS = 6
HD = 64
FF = 1536
STEP = 10

EPS_NORM = 1e-06
BETA_ONE = 0.9
BETA_TWO = 0.999
RATE_MATRIX = 0.003
RATE_VECTOR = 0.01
DECAY_MATRIX = 0.05
EPS_ADAM = 1e-08
NEG_FILL = -1e30

F32 = jnp.float32
MESH = pl.DeviceIdType.MESH
BF16 = jnp.bfloat16


def dot_nn(left, right):
    return lax.dot_general(left, right, (((1,), (0,)), ((), ())), preferred_element_type=F32)


def dot_nt(left, right):
    return lax.dot_general(left, right, (((1,), (1,)), ((), ())), preferred_element_type=F32)


def dot_tn(left, right):
    return lax.dot_general(left, right, (((0,), (0,)), ((), ())), preferred_element_type=F32)


def fold_rows(values):
    rows, cols = values.shape
    return jnp.sum(values.reshape(rows // 8, 8, cols), 0)


def loop(count, body):
    lax.fori_loop(0, count, lambda i, c: (body(i), c)[1], 0)


def gelu_pair(u):
    cdf = 0.5 + 0.5 * lax.erf(u * (0.5**0.5))
    slope = cdf + u * (jnp.exp(-0.5 * u * u) * 0.3989422804014327)
    return u * cdf, slope


class Dims:
    def __init__(self, layers, images, seq, width, halves, ranks, blocks, block_rows):
        self.layers, self.images, self.seq, self.width = layers, images, seq, width
        self.halves, self.ranks, self.blocks, self.block_rows = halves, ranks, blocks, block_rows
        self.pad_seq = -(-seq // 16) * 16
        self.tokens = images * self.pad_seq
        self.slots = blocks // ranks
        side = 1
        while side**3 * 8 <= ranks:
            side *= 2
        self.axes = (ranks // (side * side), side, side)
        self.shard_rows = -(-block_rows * self.slots // 16) * 16
        self.first_rows = -(-self.shard_rows // 32) * 16
        self.groups = block_rows // 2 if 2 * self.slots % 16 == 0 else 1
        self.group = self.shard_rows // self.groups
        self.group_js = block_rows // self.groups
        self.keys = ranks * self.group
        self.half_cols = HEADS * HD // halves
        self.half_units = FF // halves
        self.natural = 4 * self.half_cols
        self.unit_blocks = self.half_units // block_rows
        self.group_units = self.group_js * self.unit_blocks
        self.half_rows = self.natural + 2 * self.half_units


def divide(values, number):
    return jnp.floor((values.astype(F32) + 0.5) * (1.0 / number))


def one_hot(rows, codes, axis):
    start, count = rows
    shape = (count, codes.shape[1]) if axis == 0 else (codes.shape[0], count)
    here = lax.broadcasted_iota(jnp.int32, shape, axis) + start
    return (here == codes.astype(jnp.int32)).astype(F32).astype(BF16)


def permute_in(dm, layer, half, s):
    cols, units = dm.half_cols, dm.half_units
    shards = [
        s.gath[layer, :, :, :, g * dm.group : (g + 1) * dm.group, :].reshape(dm.keys, dm.width)
        for g in range(dm.groups)
    ]
    code = s.codes[layer]
    for kind in range(4):
        total = None
        for g in range(dm.groups):
            part = dot_nn(one_hot((kind * cols, cols), code[g : g + 1, :], 0), shards[g])
            total = part if total is None else total + part
        total = total.astype(BF16)
        if kind < 3:
            s.w_qkv[layer, pl.ds(pl.multiple_of(kind * HEADS * HD + half * cols, 16), cols), :] = total
        else:
            s.w_out[layer, pl.ds(pl.multiple_of(half * cols, 16), cols), :] = total
    yield
    tile = min(256, dm.group_units)
    for g in range(dm.groups):
        for target, first in ((s.w_up, 0), (s.w_down, dm.group_units)):
            for start in range(0, dm.group_units, tile):
                chosen = one_hot((first + start, tile), code[dm.groups : dm.groups + 1, :], 0)
                at = pl.multiple_of(half * units + g * dm.group_units + start, 16)
                target[layer, pl.ds(at, tile), :] = dot_nn(chosen, shards[g]).astype(BF16)


def permute_out(dm, layer, half, s):
    natural, units, size = dm.natural, dm.half_units, dm.group_units

    def summed(start, count):
        rows = slice(start, start + count)
        return (s.grads[half, rows, :].astype(F32) + s.grads_in[rows, :].astype(F32)).astype(BF16)

    qkvo = summed(0, natural)
    per = dm.axes[1] * dm.axes[2] * dm.group
    for g in range(dm.groups):
        both = jnp.concatenate(
            [summed(natural + g * size, size), summed(natural + units + g * size, size)], 0
        )
        for z in range(dm.axes[0]):
            codes = jnp.transpose(s.codes[layer, :, z * per : (z + 1) * per])
            rows = dot_nn(one_hot((0, natural), codes[:, g : g + 1], 1), qkvo)
            rows = rows + dot_nn(one_hot((0, 2 * size), codes[:, dm.groups : dm.groups + 1], 1), both)
            s.gath[layer, z, :, :, g * dm.group : (g + 1) * dm.group, :] = rows.astype(BF16).reshape(
                dm.axes[1], dm.axes[2], dm.group, dm.width
            )


def prepare_codes(dm, slot_block, s):
    layers, blocks, group = dm.layers, dm.blocks, dm.group
    block = slot_block[...].astype(F32)
    high = divide(block, 16)
    zero = jnp.zeros((16 - 2 * layers, blocks), F32)
    halves = jnp.concatenate([high, block - 16.0 * high, zero], 0).astype(BF16)
    first = dm.natural // dm.block_rows
    size = min(768, dm.keys)
    for start in range(0, dm.keys, size):
        size = min(size, dm.keys - start)

        def place(shape):
            key = lax.broadcasted_iota(jnp.int32, shape, 1) + start
            rank = divide(key, group)
            inside = key.astype(F32) - rank * group
            odd = divide(inside, dm.slots)
            return rank * dm.slots + inside - odd * dm.slots, odd, inside >= dm.group_js * dm.slots

        slot, _, _ = place((blocks, size))
        same = slot == lax.broadcasted_iota(jnp.int32, (blocks, size), 0).astype(F32)
        parts = dot_nn(halves, same.astype(F32).astype(BF16))
        _, odd, padding = place((1, size))
        for layer in range(layers):
            block = 16.0 * parts[layer : layer + 1] + parts[layers + layer : layers + layer + 1]
            rows = []
            for g in range(dm.groups):
                at = block * dm.block_rows + g * dm.group_js + odd
                rows.append(jnp.where(padding | (block >= first), -1.0, at))
            inner = block - first
            at = odd * dm.unit_blocks + inner
            at = jnp.where(inner < dm.unit_blocks, at, at - dm.unit_blocks + dm.group_units)
            rows.append(jnp.where(padding | (inner < 0), -1.0, at))
            rows.append(jnp.zeros((8 - len(rows), size), F32))
            s.codes[layer, :, start : start + size] = jnp.concatenate(rows, 0)


def unit_order(dm):
    units = dm.half_units
    here = lax.broadcasted_iota(jnp.int32, (units, units), 1)
    inner = divide(here, dm.unit_blocks)
    source = (here.astype(F32) - inner * dm.unit_blocks) * dm.block_rows + inner
    same = source == lax.broadcasted_iota(jnp.int32, (units, units), 0).astype(F32)
    return same.astype(F32).astype(BF16)


def reorder(dot, row, order):
    high = row.astype(BF16)
    rest = row - high.astype(F32)
    middle = rest.astype(BF16)
    low = (rest - middle.astype(F32)).astype(BF16)
    parts = [high.astype(F32), middle.astype(F32), low.astype(F32)]
    parts.append(jnp.zeros((13, row.shape[1]), F32))
    out = dot(jnp.concatenate(parts, 0).astype(BF16), order)
    return out[0:1] + (out[1:2] + out[2:3])


def pack_vectors(dm, vectors, first, s):
    cols, units, width = dm.half_cols, dm.half_units, dm.width
    wide = HEADS * HD
    order = unit_order(dm)
    for layer in range(dm.layers):
        rows = jnp.concatenate([vectors[0, r, layer : layer + 1, :] for r in range(6)], 0)
        flat = rows[0:1]
        q, v = flat[:, :cols], flat[:, cols : 2 * cols]
        none, mid = jnp.zeros((1, cols), F32), jnp.zeros((1, wide), F32)
        tail = jnp.zeros((1, FF - 3 * wide), F32)
        zero_half = jnp.concatenate([q, none, mid, v, none, tail], 1)
        one_half = jnp.concatenate([none, q, mid, none, v, tail], 1)
        s.vec_own[layer, 0:1, :] = jnp.where(first, zero_half, one_half)
        up = reorder(dot_nn, jnp.concatenate([rows[1:2], rows[2:3]], 1), order)
        none = jnp.zeros((1, units), F32)
        s.vec_own[layer, 1:2, :] = jnp.where(
            first, jnp.concatenate([up, none], 1), jnp.concatenate([none, up], 1)
        )
        own = jnp.concatenate([rows[3:6], jnp.zeros((3, FF - width), F32)], 1)
        none = jnp.zeros((3, FF), F32)
        s.vec_own[layer, 2:5, :] = jnp.where(first, own, none)
        s.vec_own[layer, 5:8, :] = jnp.where(first, none, own)


def unpack_vectors(dm, packed, first):
    cols, units, width = dm.half_cols, dm.half_units, dm.width
    wide = HEADS * HD
    flat = packed[0:1]
    zero_half = jnp.concatenate([flat[:, :cols], flat[:, 2 * wide : 2 * wide + cols]], 1)
    one_half = jnp.concatenate([flat[:, cols : 2 * cols], flat[:, 2 * wide + cols : 3 * wide]], 1)
    flat = packed[1:2]
    up = reorder(dot_nt, jnp.where(first, flat[:, :units], flat[:, units:]), unit_order(dm))
    own = jnp.where(first, packed[2:5, :width], packed[5:8, :width])
    return jnp.concatenate(
        [
            jnp.where(first, zero_half, one_half),
            up[:, :width],
            up[:, width:],
            own,
            jnp.zeros((2, width), F32),
        ],
        0,
    )


NORM_ROWS = 64


def norm_forward(dm, layer, source, gain, shift, low_out, hat_out, columns, place):
    def chunk(i):
        rows = pl.ds(pl.multiple_of(i * NORM_ROWS, NORM_ROWS), NORM_ROWS)
        values = source[rows, :]
        centred = values - jnp.mean(values, -1, keepdims=True)
        inv = lax.rsqrt(jnp.mean(centred * centred, -1, keepdims=True) + EPS_NORM)
        hat = centred * inv
        hat_out[layer, rows, :] = hat
        columns[rows, place : place + 1] = inv
        low_out[layer, rows, :] = (hat * gain + shift).astype(BF16)

    loop(dm.tokens // NORM_ROWS, chunk)


def norm_backward(dm, layer, grad, into, gain, hat_in, columns, place):
    def chunk(i, carry):
        rows = pl.ds(pl.multiple_of(i * NORM_ROWS, NORM_ROWS), NORM_ROWS)
        out, hat, inv = grad[rows, :], hat_in[layer, rows, :], columns[rows, place : place + 1]
        scaled = out * gain
        first = jnp.mean(scaled, -1, keepdims=True)
        second = jnp.mean(scaled * hat, -1, keepdims=True)
        into[rows, :] = into[rows, :] + inv * (scaled - first - hat * second)
        return carry[0] + fold_rows(out * hat), carry[1] + fold_rows(out)

    zero = jnp.zeros((8, dm.width), F32)
    gains, shifts = lax.fori_loop(0, dm.tokens // NORM_ROWS, chunk, (zero, zero))
    return jnp.sum(gains, 0, keepdims=True), jnp.sum(shifts, 0, keepdims=True)


def image_rows(dm, image):
    return pl.ds(pl.multiple_of(image * dm.pad_seq, 16), dm.pad_seq)


def forward_layer(dm, layer, vec, s, tick):
    width, tokens = dm.width, dm.tokens
    wide = HEADS * HD
    gain = [vec[layer, row : row + 1, :width] for row in range(2, 8)]
    g1, c1, bo, g2, c2, b2 = gain
    norm_forward(dm, layer, s.hid, g1, c1, s.low_a, s.hat_a, s.columns, 1 + 2 * layer)
    tick('norm')

    def project(image):
        rows = image_rows(dm, image)
        source = s.low_a[layer, rows, :]
        for kind in range(3):
            cols = slice(kind * wide, (kind + 1) * wide)
            value = dot_nt(source, s.w_qkv[layer, cols, :]) + vec[layer, 0:1, cols]
            s.qkv[layer, rows, cols] = value.astype(BF16)

    loop(dm.images, project)
    tick('project')

    def attend(image):
        rows = image_rows(dm, image)
        keep = s.columns[rows, 0:1]
        for head in range(HEADS):
            cols = slice(head * HD, (head + 1) * HD)
            q = s.qkv[layer, rows, cols]
            k = s.qkv[layer, rows, wide + head * HD : wide + (head + 1) * HD]
            v = s.qkv[layer, rows, 2 * wide + head * HD : 2 * wide + (head + 1) * HD]
            scores = dot_nt(k, q)
            scores = jnp.where(keep > 0, scores * HD ** (-0.5), NEG_FILL)
            exponent = jnp.exp(scores - jnp.max(scores, 0, keepdims=True))
            probs = (exponent * (1.0 / jnp.sum(exponent, 0, keepdims=True))).astype(BF16)
            s.probs[layer, image * HEADS + head] = probs
            s.att[layer, rows, cols] = dot_tn(probs, v).astype(BF16)

    loop(dm.images, attend)
    tick('attend')

    def out_project(image):
        rows = image_rows(dm, image)
        s.mid[rows, :] = s.hid[rows, :] + (dot_nn(s.att[layer, rows, :], s.w_out[layer]) + bo)

    loop(dm.images, out_project)
    norm_forward(dm, layer, s.mid, g2, c2, s.low_b, s.hat_b, s.columns, 2 + 2 * layer)
    tick('mid')

    tile = 256

    def up(image):
        rows = image_rows(dm, image)
        source = s.low_b[layer, rows, :]
        for number in range(FF // tile):
            cols = slice(number * tile, (number + 1) * tile)
            u = dot_nt(source, s.w_up[layer, cols, :]) + vec[layer, 1:2, cols]
            act, slope = gelu_pair(u)
            s.act[layer, rows, cols] = act.astype(BF16)
            s.slope[layer, rows, cols] = slope.astype(BF16)

    loop(dm.images, up)
    tick('up')

    def down(image):
        rows = image_rows(dm, image)
        s.hid[rows, :] = s.mid[rows, :] + (dot_nn(s.act[layer, rows, :], s.w_down[layer]) + b2)

    loop(dm.images, down)
    tick('down')


def low_and_sum(dm, source, target):
    def chunk(i, carry):
        rows = pl.ds(pl.multiple_of(i * NORM_ROWS, NORM_ROWS), NORM_ROWS)
        low = source[rows, :].astype(BF16)
        target[rows, :] = low
        return carry + fold_rows(low.astype(F32))

    total = lax.fori_loop(0, dm.tokens // NORM_ROWS, chunk, jnp.zeros((8, dm.width), F32))
    return jnp.sum(total, 0, keepdims=True)


def column_sums(dm, read, cols):
    def chunk(i, carry):
        rows = pl.ds(pl.multiple_of(i * NORM_ROWS, NORM_ROWS), NORM_ROWS)
        return carry + fold_rows(read(rows).astype(F32))

    total = lax.fori_loop(0, dm.tokens // NORM_ROWS, chunk, jnp.zeros((8, cols), F32))
    return jnp.sum(total, 0, keepdims=True)


def backward_layer(dm, layer, vec, vec_grad, s, tick):
    width, tokens = dm.width, dm.tokens
    wide, cols_half, units = HEADS * HD, dm.half_cols, dm.half_units
    tile = 256
    vec_grad[layer, 7:8, :width] = low_and_sum(dm, s.hid, s.low_g)
    tick("start")
    per_half = units // tile

    def unit_tile(number):
        cols = pl.ds(pl.multiple_of(number * tile, tile), tile)
        grad = dot_nt(s.low_g[...], s.w_down[layer, cols, :])
        grad = (grad * s.slope[layer, :, cols].astype(F32)).astype(BF16)
        s.slope[layer, :, cols] = grad
        half, at = number // per_half, pl.multiple_of((number % per_half) * tile, tile)
        s.grads[half, pl.ds(dm.natural + units + at, tile), :] = dot_tn(
            s.act[layer, :, cols], s.low_g[...]
        ).astype(BF16)
        s.grads[half, pl.ds(dm.natural + at, tile), :] = dot_tn(grad, s.low_b[layer]).astype(BF16)

    loop(FF // tile, unit_tile)
    tick("units")
    vec_grad[layer, 1:2, :] = column_sums(dm, lambda rows: s.slope[layer, rows, :], FF)

    def down(image):
        rows = image_rows(dm, image)
        s.mid[rows, :] = dot_nn(s.slope[layer, rows, :], s.w_up[layer])

    loop(dm.images, down)
    tick("down")
    gains, shifts = norm_backward(dm, layer, s.mid, s.hid, vec[layer, 5:6, :width], s.hat_b, s.columns, 2 + 2 * layer)
    vec_grad[layer, 5:6, :width] = gains
    vec_grad[layer, 6:7, :width] = shifts
    vec_grad[layer, 4:5, :width] = low_and_sum(dm, s.hid, s.low_g)
    tick("mid")
    value = dot_tn(s.att[layer], s.low_g[...]).astype(BF16)
    for half in range(dm.halves):
        s.grads[half, 3 * cols_half : dm.natural, :] = value[half * cols_half : (half + 1) * cols_half]

    def out_project(image):
        rows = image_rows(dm, image)
        s.att[layer, rows, :] = dot_nt(s.low_g[rows, :], s.w_out[layer]).astype(BF16)

    loop(dm.images, out_project)
    tick("out")

    def attend(image):
        rows = image_rows(dm, image)
        keep = s.columns[rows, 0:1] * HD ** (-0.5)
        for head in range(HEADS):
            cols = slice(head * HD, (head + 1) * HD)
            k_cols = slice(wide + head * HD, wide + (head + 1) * HD)
            v_cols = slice(2 * wide + head * HD, 2 * wide + (head + 1) * HD)
            q, k, v = (s.qkv[layer, rows, c] for c in (cols, k_cols, v_cols))
            out = s.att[layer, rows, cols]
            probs = s.probs[layer, image * HEADS + head]
            s.qkv[layer, rows, v_cols] = dot_nn(probs, out).astype(BF16)
            grad = dot_nt(v, out)
            wide_probs = probs.astype(F32)
            total = jnp.sum(wide_probs * grad, 0, keepdims=True)
            raw = (wide_probs * (grad - total) * keep).astype(BF16)
            s.qkv[layer, rows, cols] = dot_tn(raw, k).astype(BF16)
            s.qkv[layer, rows, k_cols] = dot_nn(raw, q).astype(BF16)

    loop(dm.images, attend)
    for kind in range(3):
        value = dot_tn(s.qkv[layer, :, kind * wide : (kind + 1) * wide], s.low_a[layer]).astype(BF16)
        for half in range(dm.halves):
            s.grads[half, kind * cols_half : (kind + 1) * cols_half, :] = value[
                half * cols_half : (half + 1) * cols_half
            ]
    tick("attend")
    vec_grad[layer, 0:1, : 3 * wide] = column_sums(dm, lambda rows: s.qkv[layer, rows, :], 3 * wide)

    def project(image):
        rows = image_rows(dm, image)
        s.mid[rows, :] = dot_nn(s.qkv[layer, rows, :], s.w_qkv[layer])

    loop(dm.images, project)
    tick("project")
    gains, shifts = norm_backward(dm, layer, s.mid, s.hid, vec[layer, 2:3, :width], s.hat_a, s.columns, 1 + 2 * layer)
    vec_grad[layer, 2:3, :width] = gains
    vec_grad[layer, 3:4, :width] = shifts
    tick("end")


class Net:
    def __init__(self, dm, s):
        self.dm, self.s, self.used = dm, s, 0
        self.rank, self.core = lax.axis_index("dp"), lax.axis_index("mp")
        _, rows, cols = dm.axes
        self.place = (self.rank // (rows * cols), (self.rank // cols) % rows, self.rank % cols)

    def device(self, axis, offset):
        if axis == 3:
            return (self.rank, 1 - self.core)
        at = list(self.place)
        at[axis] = (at[axis] + offset) % self.dm.axes[axis]
        return ((at[0] * self.dm.axes[1] + at[1]) * self.dm.axes[2] + at[2], self.core)

    def along(self, axis, offset):
        return (self.place[axis] + offset) % self.dm.axes[axis]

    def partners(self):
        found = [self.device(3, 1)]
        for axis in range(3):
            found += [self.device(axis, o) for o in range(1, self.dm.axes[axis])]
        return found

    def greet(self, semaphore):
        for partner in self.partners():
            pl.semaphore_signal(semaphore, inc=1, device_id=partner, device_id_type=MESH)

    def met(self, semaphore):
        pl.semaphore_wait(semaphore, len(self.partners()))

    def send(self, source, target, axis, offset=1):
        number = self.used
        self.used += 1
        copy = pltpu.make_async_remote_copy(
            src_ref=source,
            dst_ref=target,
            send_sem=self.s.send_sems.at[number],
            recv_sem=self.s.recv_sems.at[number],
            device_id=self.device(axis, offset),
            device_id_type=MESH,
        )
        copy.start()
        return copy


def copies_needed(dm):
    depth, rows, cols = dm.axes
    cross = depth * ((cols - 1) + (rows - 1))
    moves = depth - 1 + 2 * cross
    vectors = 1 + (depth - 1) + (rows - 1) + (cols - 1)
    return dm.layers * (2 * moves + 6 + 4 + vectors) + 2 * dm.images + 1


def gather_steps(dm, layer, net, s, sent):
    depth, rows, cols = dm.axes
    z, y, x = net.place
    buf = s.gath.at[layer]
    head, tail = pl.ds(0, dm.first_rows), pl.ds(dm.first_rows, dm.shard_rows - dm.first_rows)
    first, second, third = {}, {}, {}

    def one(offset):
        ref = buf.at[z, y, x]
        first[offset] = net.send(ref, ref, 0, offset)
        sent.append(first[offset])

    def two(piece):
        at = net.along(0, -piece)
        a, b = buf.at[at, y, x, head], buf.at[at, y, x, tail]
        second[piece] = [net.send(a, a, 2, o) for o in range(1, cols)]
        second[piece] += [net.send(b, b, 1, o) for o in range(1, rows)]
        sent.extend(second[piece])

    def three(piece):
        at = net.along(0, -piece)
        a, b = buf.at[at, y, :, head], buf.at[at, :, x, tail]
        third[piece] = [net.send(a, a, 1, o) for o in range(1, rows)]
        third[piece] += [net.send(b, b, 2, o) for o in range(1, cols)]
        sent.extend(third[piece])

    def arrived(copies):
        for copy in copies:
            copy.wait_recv()

    for offset in range(1, depth):
        one(offset)
    two(0)
    yield
    arrived(second[0])
    three(0)
    order = sorted(range(1, depth), key=lambda o: min(o, depth - o))
    for number, piece in enumerate(order):
        arrived([first[piece]])
        two(piece)
        if number > 0:
            arrived(second[order[number - 1]])
            three(order[number - 1])
        yield
    arrived(second[order[-1]])
    three(order[-1])
    yield
    for piece in range(depth):
        arrived(third[piece])


def scatter_steps(dm, layer, net, s, sent):
    depth, rows, cols = dm.axes
    z, y, x = net.place
    buf = s.gath.at[layer]
    head, tail = pl.ds(0, dm.first_rows), pl.ds(dm.first_rows, dm.shard_rows - dm.first_rows)
    order = sorted(range(depth), key=lambda o: -min(o, depth - o))
    first, second, third = {}, {}, {}

    def add(at, parts):
        value = buf[at].astype(F32)
        for part in parts:
            value = value + part.astype(F32)
        buf[at] = value.astype(BF16)

    for piece in order:
        at = net.along(0, piece)
        a, b = [], []
        for o in range(1, rows):
            to = net.along(1, o)
            a.append(net.send(buf.at[at, to, :, head], s.one_a.at[piece, o - 1], 1, o))
        for o in range(1, cols):
            to = net.along(2, o)
            b.append(net.send(buf.at[at, :, to, tail], s.one_b.at[piece, o - 1], 2, o))
        first[piece] = (a, b)
        sent.extend(a + b)
    yield
    for piece in order:
        at = net.along(0, piece)
        for copy in first[piece][0] + first[piece][1]:
            copy.wait_recv()
        add((at, y, slice(None), head), [s.one_a[piece, o] for o in range(rows - 1)])
        add((at, slice(None), x, tail), [s.one_b[piece, o] for o in range(cols - 1)])
        a, b = [], []
        for o in range(1, cols):
            to = net.along(2, o)
            a.append(net.send(buf.at[at, y, to, head], s.two_a.at[piece, o - 1], 2, o))
        for o in range(1, rows):
            to = net.along(1, o)
            b.append(net.send(buf.at[at, to, x, tail], s.two_b.at[piece, o - 1], 1, o))
        second[piece] = (a, b)
        sent.extend(a + b)
        yield
    for piece in order:
        at = net.along(0, piece)
        for copy in second[piece][0] + second[piece][1]:
            copy.wait_recv()
        add((at, y, x, head), [s.two_a[piece, o] for o in range(cols - 1)])
        add((at, y, x, tail), [s.two_b[piece, o] for o in range(rows - 1)])
        if piece > 0:
            third[piece] = net.send(buf.at[at, y, x], s.three.at[piece - 1], 0, piece)
            sent.append(third[piece])
        yield
    value = buf[z, y, x].astype(F32)
    for piece in range(1, depth):
        third[piece].wait_recv()
        value = value + s.three[piece - 1].astype(F32)
    s.rows[...] = value


def vector_steps(dm, layer, net, s, first, sent):
    copy = net.send(s.vec_grad.at[layer], s.vec_back.at[layer], 3)
    sent.append(copy)
    yield
    copy.wait_recv()
    value = unpack_vectors(dm, s.vec_grad[layer] + s.vec_back[layer], first)
    for axis, buf in ((1, s.vec_y), (2, s.vec_x), (0, s.vec_z)):
        here = net.place[axis]
        buf[layer, here] = value
        copies = []
        for o in range(1, dm.axes[axis]):
            copies.append(net.send(buf.at[layer, here], buf.at[layer, here], axis, o))
        sent.extend(copies)
        yield
        for copy in copies:
            copy.wait_recv()
        value = buf[layer, 0]
        for o in range(1, dm.axes[axis]):
            value = value + buf[layer, o]
    s.vec_sum[layer] = value


class Refs:
    pass


def scratch_shapes(dm):
    layers, tokens, width, wide = dm.layers, dm.tokens, dm.width, HEADS * HD
    depth, rows, cols = dm.axes
    head, tail = dm.first_rows, dm.shard_rows - dm.first_rows
    vmem, copies = pltpu.VMEM, copies_needed(dm)
    return dict(
        hid=vmem((tokens, width), F32),
        mid=vmem((tokens, width), F32),
        columns=vmem((tokens, 8), F32),
        low_a=vmem((layers, tokens, width), BF16),
        low_b=vmem((layers, tokens, width), BF16),
        low_g=vmem((tokens, width), BF16),
        hat_a=vmem((layers, tokens, width), F32),
        hat_b=vmem((layers, tokens, width), F32),
        qkv=vmem((layers, tokens, 3 * wide), BF16),
        probs=vmem((layers, dm.images * HEADS, dm.pad_seq, dm.pad_seq), BF16),
        att=vmem((layers, tokens, wide), BF16),
        act=vmem((layers, tokens, FF), BF16),
        slope=vmem((layers, tokens, FF), BF16),
        w_qkv=vmem((layers, 3 * wide, width), BF16),
        w_out=vmem((layers, wide, width), BF16),
        w_up=vmem((layers, FF, width), BF16),
        w_down=vmem((layers, FF, width), BF16),
        grads=vmem((dm.halves, dm.half_rows, width), BF16),
        grads_in=vmem((dm.half_rows, width), BF16),
        gath=vmem((layers, depth, rows, cols, dm.shard_rows, width), BF16),
        one_a=vmem((depth, rows - 1, cols, head, width), BF16),
        one_b=vmem((depth, cols - 1, rows, tail, width), BF16),
        two_a=vmem((depth, cols - 1, head, width), BF16),
        two_b=vmem((depth, rows - 1, tail, width), BF16),
        three=vmem((depth - 1, dm.shard_rows, width), BF16),
        rows=vmem((dm.shard_rows, width), F32),
        tok_in=vmem((dm.images, dm.seq, width), F32),
        tok_out=vmem((dm.images, dm.seq, width), F32),
        codes=vmem((layers, 8, dm.keys), F32),
        vec_own=vmem((layers, 8, FF), F32),
        vec=vmem((layers, 8, FF), F32),
        vec_grad=vmem((layers, 8, FF), F32),
        vec_in=vmem((layers, 8, FF), F32),
        vec_back=vmem((layers, 8, FF), F32),
        vec_z=vmem((layers, depth, 8, width), F32),
        vec_y=vmem((layers, rows, 8, width), F32),
        vec_x=vmem((layers, cols, 8, width), F32),
        vec_sum=vmem((layers, 8, width), F32),
        keep_row=vmem((8, -(-dm.pad_seq // 128) * 128), F32),
        send_sems=pltpu.SemaphoreType.DMA((copies,)),
        recv_sems=pltpu.SemaphoreType.DMA((copies,)),
        local_sems=pltpu.SemaphoreType.DMA((4 * dm.images,)),
        credit=pltpu.SemaphoreType.REGULAR,
    )


def load_tokens(dm, source, target, scale=None):
    tail = dm.pad_seq - 16
    for image in range(dm.images):
        start = image * dm.pad_seq
        target[start + tail : start + dm.pad_seq, :] = jnp.zeros((16, dm.width), F32)
        value = source[image]
        if scale is not None:
            value = value * scale[start : start + dm.seq, 0:1]
        target[start : start + dm.seq, :] = value


class Tokens:
    def __init__(self, dm, net, s):
        self.dm, self.net, self.s, self.used = dm, net, s, 0

    def image(self, ref, number):
        return ref.at[:, self.net.core * self.dm.images + number]

    def start(self, source, target):
        copy = pltpu.make_async_copy(source, target, self.s.local_sems.at[self.used])
        self.used += 1
        copy.start()
        return copy

    def load(self, ref):
        return [self.start(self.image(ref, i), self.s.tok_in.at[i]) for i in range(self.dm.images)]

    def store(self, ref):
        copies = []
        for i in range(self.dm.images):
            copies.append(self.start(self.s.tok_out.at[i], self.image(ref, i)))
            copies.append(self.net.send(self.s.tok_out.at[i], self.image(ref, i), 3))
        return copies


def wait_all(copies):
    for copy in copies:
        copy.wait()


def prepare_keep(dm, keep_mask, first, s):
    kept = keep_mask[...].astype(F32)
    kept = jnp.where(first, kept[: dm.images], kept[dm.images :])
    s.keep_row[...] = jnp.zeros(s.keep_row.shape, F32)
    s.keep_row[: dm.images, : dm.seq] = kept
    columns = jnp.transpose(s.keep_row[...])
    for image in range(dm.images):
        rows = slice(image * dm.pad_seq, (image + 1) * dm.pad_seq)
        s.columns[rows, 0:1] = columns[: dm.pad_seq, image : image + 1]


def own_shard(dm, master, net, s):
    z, y, x = net.place
    if dm.shard_rows > dm.block_rows * dm.slots:
        s.rows[...] = jnp.zeros(s.rows.shape, F32)
    for layer in range(dm.layers):
        for j in range(dm.block_rows):
            s.rows[j * dm.slots : (j + 1) * dm.slots, :] = master[0, layer, j]
        s.gath[layer, z, y, x] = s.rows[...].astype(BF16)


def step_kernel(dm, names, hidden, keep_mask, cotangent, slot_block, master, vectors, acts, grad_in, matrix, vec_out, *scratch):
    s = Refs()
    for name, ref in zip(names, scratch):
        setattr(s, name, ref)
    net = Net(dm, s)
    first = net.core == 0
    tokens = Tokens(dm, net, s)
    sent = []
    barrier = pltpu.get_barrier_semaphore()
    net.greet(barrier)
    load = tokens.load(hidden)
    own_shard(dm, master, net, s)
    net.met(barrier)
    moved = [[] for _ in range(dm.layers)]
    gathers = [gather_steps(dm, 0, net, s, moved[0])]
    next(gathers[0])
    pack_vectors(dm, vectors, first, s)
    other_vec = net.send(s.vec_own, s.vec_in, 3)
    sent.append(other_vec)
    prepare_codes(dm, slot_block, s)
    prepare_keep(dm, keep_mask, first, s)
    wait_all(load)
    load_tokens(dm, s.tok_in, s.hid)
    load = tokens.load(cotangent)
    other_vec.wait_recv()
    s.vec[...] = s.vec_own[...] + s.vec_in[...]
    for _ in gathers[0]:
        pass

    def share(layer):
        cols, units = dm.half_cols, dm.half_units
        parts = permute_in(dm, layer, net.core, s)
        copies = []

        def push(ref, start, count):
            rows = ref.at[layer, pl.ds(pl.multiple_of(start, 16), count)]
            copies.append(net.send(rows, rows, 3))

        for _ in parts:
            for kind in range(3):
                push(s.w_qkv, kind * HEADS * HD + net.core * cols, cols)
            push(s.w_out, net.core * cols, cols)
        push(s.w_up, net.core * units, units)
        push(s.w_down, net.core * units, units)
        sent.extend(copies)
        return copies

    weights = share(0)
    for layer in range(dm.layers):
        following = []
        if layer + 1 < dm.layers:
            following = gather_steps(dm, layer + 1, net, s, moved[layer + 1])

        def tick(name):
            if name == "norm":
                for copy in weights[:3]:
                    copy.wait_recv()
            if name == "attend":
                weights[3].wait_recv()
            if name == "mid":
                weights[4].wait_recv()
            if name == "up":
                weights[5].wait_recv()
            if following:
                next(following, None)

        forward_layer(dm, layer, s.vec, s, tick)
        if following:
            for _ in following:
                pass
            weights = share(layer + 1)
    for image in range(dm.images):
        rows = slice(image * dm.pad_seq, image * dm.pad_seq + dm.seq)
        s.tok_out[image] = s.hid[rows, :] * s.columns[rows, 0:1]
    store = tokens.store(acts)
    wait_all(load)
    load_tokens(dm, s.tok_in, s.hid, s.columns)

    pending = []

    def advance(count):
        for _ in range(count):
            for steps in pending:
                next(steps, None)

    def finish(layer):
        for steps in pending:
            for _ in steps:
                pass
        pending.clear()
        for j in range(dm.block_rows):
            matrix[0, layer, j] = s.rows[j * dm.slots : (j + 1) * dm.slots, :]
        for r in range(vec_out.shape[1]):
            vec_out[0, r, layer : layer + 1, :] = s.vec_sum[layer, r : r + 1, :]

    for layer in reversed(range(dm.layers)):
        last = layer == 0
        shared = []

        def push(start, count):
            rows = pl.ds(start, count)
            shared.append(net.send(s.grads.at[1 - net.core, rows], s.grads_in.at[rows], 3))

        def tick(name):
            if name == "units":
                if layer + 1 < dm.layers:
                    finish_credit()
                push(dm.natural, 2 * dm.half_units)
            if name == "attend":
                push(0, dm.natural)
            if name == "attend" and last:
                scatter()
            if name in ("start", "down", "mid", "out", "project"):
                advance(2)

        def scatter():
            for copy in shared:
                copy.wait_recv()
            for copy in moved[layer]:
                copy.wait_send()
            permute_out(dm, layer, net.core, s)
            pending.append(scatter_steps(dm, layer, net, s, sent))
            advance(1)

        def finish_credit():
            finish(layer + 1)
            net.greet(s.credit)
            net.met(s.credit)

        backward_layer(dm, layer, s.vec, s.vec_grad, s, tick)
        for copy in shared:
            copy.wait_send()
        if not last:
            scatter()
        pending.append(vector_steps(dm, layer, net, s, first, sent))
        advance(1)
    wait_all(store)
    for image in range(dm.images):
        rows = slice(image * dm.pad_seq, image * dm.pad_seq + dm.seq)
        s.tok_out[image] = s.hid[rows, :]
    store = tokens.store(grad_in)
    finish(0)
    wait_all(store)
    for copy in sent:
        copy.wait_send()
    assert net.used <= copies_needed(dm)


def run_step(dm, hidden_in, keep_mask, cotangent, slot_block, master, vector_master):
    shapes = scratch_shapes(dm)
    out_shape = (
        jax.ShapeDtypeStruct(hidden_in.shape, F32),
        jax.ShapeDtypeStruct(hidden_in.shape, F32),
        jax.ShapeDtypeStruct(master.shape, F32),
        jax.ShapeDtypeStruct(vector_master.shape, F32),
    )
    full, far = pl.BlockSpec(memory_space=pltpu.VMEM), pl.BlockSpec(memory_space=pl.ANY)
    return pl.pallas_call(
        functools.partial(step_kernel, dm, tuple(shapes)),
        out_shape=out_shape,
        in_specs=[far, full, far, full, full, full],
        out_specs=[far, far, full, full],
        scratch_shapes=list(shapes.values()),
        compiler_params=pltpu.CompilerParams(
            vmem_limit_bytes=63 * 2**20, collective_id=0, has_side_effects=True
        ),
    )(hidden_in, keep_mask, cotangent, slot_block, master, vector_master)


def adam_step(weight, grad_sum, first_old, second_old, rate, decay):
    first_new = BETA_ONE * first_old + (1.0 - BETA_ONE) * grad_sum
    second_new = BETA_TWO * second_old + (1.0 - BETA_TWO) * grad_sum * grad_sum
    first_hat = first_new / (1.0 - BETA_ONE**STEP)
    second_hat = second_new / (1.0 - BETA_TWO**STEP)
    return (
        second_new,
        weight - rate * (first_hat / (jnp.sqrt(second_hat) + EPS_ADAM) + decay * weight),
    )


def shards(
    hidden_in, keep_mask, cotangent, slot_block, master, moment_one, moment_two, vector_master, vector_one, vector_two
):
    images, seq, width = hidden_in.shape
    halves, ranks = lax.axis_size("mp"), lax.axis_size("dp")
    dm = Dims(
        master.shape[1], images // halves, seq, width, halves, ranks, slot_block.shape[1], master.shape[3]
    )
    activations, input_grad, matrix_grad, vector_grad = run_step(
        dm,
        hidden_in.swapaxes(0, 1),
        keep_mask,
        cotangent.swapaxes(0, 1),
        slot_block,
        master.swapaxes(2, 3),
        vector_master.swapaxes(1, 2),
    )
    activations, input_grad = activations.swapaxes(0, 1), input_grad.swapaxes(0, 1)
    matrix_grad, vector_grad = matrix_grad.swapaxes(2, 3), vector_grad.swapaxes(1, 2)
    matrix_two, matrix_new = adam_step(
        master, matrix_grad, moment_one, moment_two, RATE_MATRIX, DECAY_MATRIX
    )
    vector_two_new, vector_new = adam_step(
        vector_master, vector_grad, vector_one, vector_two, RATE_VECTOR, 0.0
    )
    return (
        activations,
        input_grad,
        matrix_grad,
        matrix_two,
        matrix_new,
        vector_grad,
        vector_two_new,
        vector_new,
    )


def solution(mesh):
    images, rows, copied = P("dp", None, None), P("mp", None, "dp", None, None), P("mp", None, None, None)
    return jax.shard_map(
        shards,
        mesh=mesh,
        in_specs=(images, P("dp", None), images, P(), rows, rows, rows, copied, copied, copied),
        out_specs=(images, images, rows, rows, rows, copied, copied, copied),
        check_vma=False,
    )
```

time: 706 us -> 208 us (0.29); the launches traced: 695 us -> 208 us
  Pallas kernels: 0 us -> 198 us
  local copies, waits for them, and re-layouts: 202 us -> 5.4 us
  waiting for transfers between devices: 187 us -> 0 us
  matrix products: 142 us -> 0 us
  blocking collectives: 80.1 us -> 0 us
  other arithmetic: 65.8 us -> 3.93 us
  between operations: 15.6 us -> 0.72 us
    pallas_call x0 -> x1, Pallas kernels: none -> 198 us  [run_step(): pl.pallas_call(functools.partial(step_kernel, dm, tuple(shapes)), out_sha...]
    dot_general x36 -> x0, matrix products: 142 us -> none  [the longest x8 42.3 us: contract_cols(): lax.dot_general(left, right, (((1,), (1,)), ((), ())), preferred_element_...]
    psum x7 -> x0, waiting for transfers between devices: 101 us -> none  [the longest x2 33.8 us: shards(): grad_normed_b = lax.psum(partial_mlp, 'mp')]
    psum x1 -> x0, blocking collectives: 78.2 us -> none  [shards(): vector_grad = lax.psum(jnp.stack(vector_grads, 0)[None], 'dp')]
    reduce_scatter x1 -> x0, waiting for transfers between devices: 56.7 us -> none  [shards(): lax.psum_scatter(whole[None], 'dp', scatter_dimension=2, tiled=True)]
    reshape x20 -> x0, local copies, waits for them, and re-layouts: 39.2 us -> none  [the longest x2 5.78 us: attention_inner(): keys_low = projected[:, head_cols:2 * head_cols].astype(jnp.bfloat16).res...]
    reduce_sum x16 -> x0, other arithmetic: 37.8 us -> none  [the longest x4 16.1 us: norm_back(): return (grad_in, jnp.sum(grad_out * normed, 0), jnp.sum(grad_out, 0))]
    scatter x1 -> x0, local copies, waits for them, and re-layouts: 36.3 us -> none  [shards(): inverse = jnp.zeros((layers, blocks), jnp.int32).at[layer_ids, slot_block...]
  transfers between devices with their start and end apart: 9 -> 0, of which waited for: 8 -> 0; matrix products, arithmetic and copies ran while one was open for 22% -> 0% of each run, Pallas kernels for 0% -> 0%
where the time goes in v1:
time: 208 us
  Pallas kernels  198 us (95%)
  local copies, waits for them, and re-layouts  5.4 us (3%)
  other arithmetic  3.93 us (2%)
    pallas_call x1, Pallas kernels, run_step(): pl.pallas_call(functools.partial(step_kernel, dm, tuple(shapes)), out_sha...  198 us
    unnamed x22, local copies, waits for them, and re-layouts  5.4 us

profile of v1, /device:TPU:0, one launch (start us, length us, event | category | flops | bytes accessed | tf_op | source)
XLA Modules:
  0.0 208.3 jit_solution(1515370789612400619)
XLA Ops:
  0.6 0.0 copy-start.5
  0.6 0.0 copy-start.7
  0.7 0.0 copy-start.8
  0.7 0.0 copy-start.2
  0.7 0.0 copy-start.4
  0.7 198.2 %shard_map.161 = (f32[198,8,384]{2,1,0:T(8,128)}, f32[198,8,384]{2,1,0:T(8,128)}, f32[1,2,6,24,384]{4,3,2,1,0:T(8,128)}, f32[1,6,2,384]{3,2,1,0:T(2,128)}) custom-call(f32[198,8,384]{2,1,0:T(8,128)} %bitcast.10, s32[8,198]{1,0:T(8,128)} %keep_mask.1, f32[198,8,384]{2,1,0:T(8,128)} %bitcast.11, s32[2,384]{1,0:T(2,128)} %slot_block.1, ...), custom_call_target="tpu_custom_call" | custom-call | tf_op jit(solution)/shard_map/pallas_call | solution.py:910
  198.9 0.0 copy-start.1
  198.9 0.0 copy-done.5
  198.9 0.0 copy-done.7
  198.9 0.0 copy-done.8
  199.0 1.6 multiply_subtract_fusion.1
  200.5 0.0 copy-done.2
  200.5 0.0 copy-done.4
  200.5 2.4 %multiply_subtract_fusion = (f32[1,2,24,6,384]{4,2,3,1,0:T(8,128)}, f32[1,2,24,6,384]{4,2,3,1,0:T(8,128)}) fusion(f32[1,2,24,6,384]{4,2,3,1,0:T(8,128)S(1)} %copy-done.2, f32[1,2,24,6,384]{4,2,3,1,0:T(8,128)S(1)} %copy-done.4, f32[1,2,24,6,384]{4,2,3,1,0:T(8,128)} %param.16, f32[1,2,6,24,384]{4,3,2,1,0:T(8,128)} %get-tuple-element.14), kind=kLoop, calls=%fused_computation.2 | loop fusion | flops 1658880 | bytes 2654208 | tf_op jit(solution)/shard_map/sub | solution.py:929
  202.9 0.0 copy-done.1
  202.9 0.0 copy-start
  202.9 1.4 copy.22
  204.3 1.1 copy-done
  205.5 0.0 copy-start.3
  205.5 1.4 copy.23
  206.9 0.0 copy-done.3
  206.9 0.8 copy.24
  207.7 0.0 copy-done.6
  207.7 0.6 copy.25
  (1 shorter events, 0.0 us)
Async XLA Ops:
  0.6 198.3 %copy-start.5 = (f32[1,2,6,384]{3,1,2,0:T(2,128)S(1)}, f32[1,2,6,384]{3,1,2,0:T(2,128)}, u32[]{:S(2)}) copy-start(f32[1,2,6,384]{3,1,2,0:T(2,128)} %param.17) | copy-start | bytes 55300
  0.6 198.3 %copy-start.7 = (f32[1,2,6,384]{3,1,2,0:T(2,128)S(1)}, f32[1,2,6,384]{3,1,2,0:T(2,128)}, u32[]{:S(2)}) copy-start(f32[1,2,6,384]{3,1,2,0:T(2,128)} %param.18) | copy-start | bytes 55300
  0.7 198.3 %copy-start.8 = (f32[1,2,6,384]{3,1,2,0:T(2,128)S(1)}, f32[1,2,6,384]{3,1,2,0:T(2,128)}, u32[]{:S(2)}) copy-start(f32[1,2,6,384]{3,1,2,0:T(2,128)} %param.19) | copy-start | bytes 55300
  0.7 199.8 %copy-start.2 = (f32[1,2,24,6,384]{4,2,3,1,0:T(8,128)S(1)}, f32[1,2,24,6,384]{4,2,3,1,0:T(8,128)}, u32[]{:S(2)}) copy-start(f32[1,2,24,6,384]{4,2,3,1,0:T(8,128)} %param.14) | copy-start | bytes 1327108
  0.7 199.8 %copy-start.4 = (f32[1,2,24,6,384]{4,2,3,1,0:T(8,128)S(1)}, f32[1,2,24,6,384]{4,2,3,1,0:T(8,128)}, u32[]{:S(2)}) copy-start(f32[1,2,24,6,384]{4,2,3,1,0:T(8,128)} %param.15) | copy-start | bytes 1327108
  198.9 4.0 %copy-start.1 = (f32[198,8,384]{2,1,0:T(8,128)S(1)}, f32[198,8,384]{2,1,0:T(8,128)}, u32[]{:S(2)}) copy-start(f32[198,8,384]{2,1,0:T(8,128)} %get-tuple-element.12) | copy-start | bytes 7299076
  202.9 2.6 %copy-start = (f32[198,8,384]{2,1,0:T(8,128)S(1)}, f32[198,8,384]{2,1,0:T(8,128)}, u32[]{:S(2)}) copy-start(f32[198,8,384]{2,1,0:T(8,128)} %get-tuple-element.13) | copy-start | bytes 7299076
  205.5 1.4 copy-start.3
  205.5 2.2 %copy-start.6 = (f32[1,6,2,384]{3,2,1,0:T(2,128)S(1)}, f32[1,6,2,384]{3,2,1,0:T(2,128)}, u32[]{:S(2)}) copy-start(f32[1,6,2,384]{3,2,1,0:T(2,128)} %get-tuple-element.15) | copy-start | bytes 55300
